TPU v7x, 32 devices: a whole 2x2x4 slice. The times are simulated.
32 devices in a mesh: runs: 2 (over x), area: 16 (over z, y, core).
Axes of the slice: x: 2, y: 2, z: 4, core: 2. Of those that a mesh axis runs over, the one named last changes fastest.
Arguments:
- history: bfloat16 [4, 32, 16384], P(None, 'runs', 'area'), parts along dimension 1, may hold values from 0 to 1
- drive: bfloat16 [32, 16384], P('runs', 'area'), parts along dimension 0, may hold values from -6 to 6
- leak: float32 [32768], P(('runs', 'area')), parts along dimension 0, may hold values from 0.1 to 0.9
- inhibition: float32 [16], P('runs'), parts along dimension 0, may hold values from 0.5 to 4
- section: int32 [16], replicated, may hold values from 0 to 7, never falling along the last dimension, each value on 1 to 6 neighbouring positions
- link_source: int32 [768, 1], P('area'), may hold values from 0 to 15; in each aligned block of 48 rows (0 to 47, 48 to 95, ...) at most 3 rows name the same one
- link_block: int32 [768], P('area'), may hold values from 0 to 3
- link_target: int32 [768], P('area'), may hold values from 0 to 3
- link_delay: int32 [768], P('area'), may hold values from 2 to 4
- remote_weight: bfloat16 [1536, 256, 256], P(('runs', 'area')), parts along dimension 0, may hold values from -0.375 to 0.375
- local_block: int32 [256], P('area'), may hold values from 0 to 3
- local_target: int32 [256], P('area'), may hold values from 0 to 3
- local_delay: int32 [256], P('area'), may hold values from 1 to 4
- local_weight: bfloat16 [512, 256, 256], P(('runs', 'area')), parts along dimension 0, may hold values from -0.375 to 0.375
Outputs:
- rates: bfloat16 [32, 16384], P('runs', 'area'), parts along dimension 0
There are 2 independent parts, one for each index of `runs`. A program takes and returns all parts, laid end to end along the dimension named above; an argument that names none is the same for every part. Nothing has to cross between parts.
Inputs may be any that keep to these rules, and one draw needn't show every extreme that they name: `section`: Nondecreasing; every area covers 1 to 6 consecutive indices, and some area covers exactly 6. `link_source`: among the 48 remote tiles of one index of area, no index of area is named more than 3 times, a bound that some block reaches.
All inputs are finite; a program needn't handle non-finite values.
Results may differ from a plain program's by a relative error of at most 0.005.
Values may be sent and summed in bfloat16 or wider, within the bound.
A program may use at most 128 MiB of HBM per device.

v0:
```python
import jax
import jax.numpy as jnp
from jax import lax
from jax.sharding import PartitionSpec as P

STEPS = 6


def local(
    history,
    drive,
    leak,
    inhibition,
    section,
    link_source,
    link_block,
    link_target,
    link_delay,
    remote_weight,
    local_block,
    local_target,
    local_delay,
    local_weight,
):
    delay_depth, trials, row_width = history.shape
    pop_size = remote_weight.shape[1]
    blocks = row_width // pop_size
    link_count = link_block.shape[0]
    devices = lax.axis_size("area")
    capacity = max(2, (link_count + devices - 1) // devices)
    slot_total = devices * capacity
    area_total = inhibition.shape[0]
    state_rows = (
        history.reshape(delay_depth, trials, blocks, pop_size)
        .transpose(0, 2, 1, 3)
        .reshape(delay_depth * blocks, trials, pop_size)
    )
    source = link_source[:, 0]
    positions = jnp.arange(link_count, dtype=jnp.int32)
    earlier = (source[:, None] == source[None, :]) & (positions[None, :] < positions[:, None])
    slot_rank = jnp.sum(earlier.astype(jnp.int32), axis=1)
    slot_index = source * capacity + slot_rank
    slot_table = slot_index[:, None] == jnp.arange(slot_total, dtype=jnp.int32)[None, :]
    slot_used = jnp.any(slot_table, axis=0)
    want_block = jnp.sum(jnp.where(slot_table, link_block[:, None], 0), axis=0)
    want_delay = jnp.where(
        slot_used, jnp.sum(jnp.where(slot_table, link_delay[:, None], 0), axis=0), delay_depth
    )
    asked_block, asked_delay = (
        lax.all_to_all(
            want_block.reshape(devices, capacity), "area", split_axis=0, concat_axis=0, tiled=True
        ),
        lax.all_to_all(
            want_delay.reshape(devices, capacity), "area", split_axis=0, concat_axis=0, tiled=True
        ),
    )
    asked_block = asked_block.reshape(slot_total)
    asked_delay = asked_delay.reshape(slot_total)
    target_onehot = (link_target[None, :] == jnp.arange(blocks, dtype=jnp.int32)[:, None]).astype(
        jnp.float32
    )
    local_onehot = (local_target[None, :] == jnp.arange(blocks, dtype=jnp.int32)[:, None]).astype(
        jnp.float32
    )
    local_index = (local_delay - 1) * blocks + local_block
    leak_rows = leak.reshape(blocks, pop_size)[:, None, :]
    drive_blocks = drive.astype(jnp.float32).reshape(trials, blocks, pop_size).transpose(1, 0, 2)
    my_index = lax.axis_index("area")
    my_area = lax.dynamic_slice_in_dim(section, my_index, 1, 0)[0]
    area_mask = jnp.arange(area_total, dtype=jnp.int32) == my_area
    area_count = jnp.sum((section == my_area).astype(jnp.float32)) * row_width
    inhibit = jnp.sum(jnp.where(area_mask, inhibition, 0.0))
    fresh = state_rows[:blocks]
    for step_index in range(STEPS):
        outgoing = jnp.take(state_rows, (asked_delay - 1) * blocks + asked_block, axis=0).reshape(
            devices, capacity, trials, pop_size
        )
        received = lax.all_to_all(
            outgoing, "area", split_axis=0, concat_axis=0, tiled=True
        ).reshape(slot_total, trials, pop_size)
        remote_in = jnp.take(received, slot_index, axis=0)
        previous = state_rows[:blocks].astype(jnp.float32)
        own_sum = jnp.sum(previous, axis=(0, 2))
        area_table = jnp.where(area_mask[:, None], own_sum[None, :], 0.0)
        summed = lax.psum(area_table, "area")
        total_mine = jnp.sum(jnp.where(area_mask[:, None], summed, 0.0), axis=0)
        mean_now = total_mine / area_count
        local_in = jnp.take(state_rows, local_index, axis=0)
        local_terms = jnp.einsum(
            "ltp,lpq->ltq", local_in, local_weight, preferred_element_type=jnp.float32
        )
        remote_terms = jnp.einsum(
            "ltp,lpq->ltq", remote_in, remote_weight, preferred_element_type=jnp.float32
        )
        current = jnp.einsum(
            "bl,ltq->btq", target_onehot, remote_terms, precision=lax.Precision.HIGHEST
        )
        current = current + jnp.einsum(
            "bl,ltq->btq", local_onehot, local_terms, precision=lax.Precision.HIGHEST
        )
        driven = jax.nn.sigmoid(current + drive_blocks - inhibit * mean_now[None, :, None])
        fresh = ((1.0 - leak_rows) * previous + leak_rows * driven).astype(jnp.bfloat16)
        state_rows = jnp.concatenate([fresh, state_rows[:-blocks]], axis=0)
    return fresh.transpose(1, 0, 2).reshape(trials, row_width)


def solution(mesh):
    placed = (
        P(None, "runs", "area"),
        P("runs", "area"),
        P(("runs", "area")),
        P("runs"),
        P(),
        P("area", None),
        P("area"),
        P("area"),
        P("area"),
        P(("runs", "area"), None, None),
        P("area"),
        P("area"),
        P("area"),
        P(("runs", "area"), None, None),
    )
    return jax.shard_map(
        local, mesh=mesh, in_specs=placed, out_specs=P("runs", "area"), check_vma=False
    )
```

profile of v0, /device:TPU:0, one launch (start us, length us, event | category | flops | bytes accessed | tf_op | source)
XLA Modules:
  0.0 361.1 jit_solution(18329687779567038272)
XLA Ops:
  0.0 1.0 convert_reduce_fusion.5
  1.0 0.7 fusion.130
  1.7 0.8 select_reduce_fusion.1
  2.4 0.7 all_to_all.29
  3.1 7.4 %all-to-all-start.1 = ((s32[16,1,3]{2,1,0:T(1,128)}), s32[16,1,3]{2,1,0:T(1,128)S(1)}, u32[]{:S(2)}, u32[]{:S(2)}) async-start(s32[16,1,3]{2,1,0:T(1,128)} %bitcast.6), calls=%async_computation.1 | async-start | bytes 16384 | tf_op jit(solution)/shard_map/all_to_all | solution.py:50
  10.6 0.7 compare_and_fusion.1
  11.3 0.8 fusion.155
  12.3 1.3 dynamic_slice.3
  13.6 0.7 iota_compare_fusion.4
  14.3 2.0 select_reduce_fusion.8
  16.3 0.7 compare_and_fusion
  17.0 0.7 broadcast_in_dim_reshape.3
  17.9 33.8 %psum.42 = f32[8,16]{1,0:T(8,128)S(1)} all-reduce(f32[8,16]{1,0:T(8,128)S(1)} %broadcast_select_fusion.11), channel_id=1, replica_groups=mesh['runs'=2,'area'=16] {'area'}, use_global_device_ids=true, to_apply=%region_7.11 | all-reduce | flops 128 | bytes 1024 | tf_op jit(solution)/shard_map/psum | solution.py:85
  51.8 1.9 fusion.129
  53.8 0.7 select_n.89
  54.4 3.5 all-to-all-start
  58.0 0.8 reshape.174
  59.9 4.4 %all-to-all-done = s32[16,1,3]{2,1,0:T(1,128)S(1)} async-done(((s32[16,1,3]{2,1,0:T(1,128)}), s32[16,1,3]{2,1,0:T(1,128)S(1)}, u32[]{:S(2)}, u32[]{:S(2)}) %all-to-all-start) | async-done | bytes 224 | tf_op jit(solution)/shard_map/all_to_all | solution.py:53
  64.5 0.6 gather_fusion
  65.1 0.9 broadcast_select_fusion.5
  65.9 3.6 all-to-all-start.2
  69.5 0.6 divide_multiply_fusion.5
  70.6 1.0 fusion.88
  71.6 10.1 %all-to-all-done.2 = bf16[16,3,16,256]{3,2,1,0:T(8,128)(2,1)S(1)} async-done(((bf16[16,3,16,256]{3,2,1,0:T(8,128)(2,1)}), bf16[16,3,16,256]{3,2,1,0:T(8,128)(2,1)S(1)}, u32[]{:S(2)}, u32[]{:S(2)}) %all-to-all-start.2) | async-done | bytes 393248 | tf_op jit(solution)/shard_map/all_to_all | solution.py:78
  82.2 3.8 %fusion.70 = f32[48,16,256]{2,1,0:T(8,128)S(1)} fusion(bf16[48,256,256]{2,1,0:T(8,128)(2,1)} %param.29, bf16[48,16,256]{2,1,0:T(8,128)(2,1)S(1)} %gather_fusion.1, pred[48]{0:T(512)(128)(4,1)S(1)} %get-tuple-element.10), kind=kOutput, calls=%fused_computation.94 | convolution fusion | flops 100859904 | bytes 7471152 | tf_op jit(solution)/shard_map/ltp,lpq->ltq/dot_general | solution.py:92
  86.0 1.0 convert_reduce_fusion.4
  88.3 31.4 %psum.43 = f32[8,16]{1,0:T(8,128)S(1)} all-reduce(f32[8,16]{1,0:T(8,128)S(1)} %broadcast_select_fusion.10), channel_id=1, replica_groups=mesh['runs'=2,'area'=16] {'area'}, use_global_device_ids=true, to_apply=%region_11.15 | all-reduce | flops 128 | bytes 1024 | tf_op jit(solution)/shard_map/psum | solution.py:85
  119.8 0.9 broadcast_select_fusion.4
  120.7 3.6 all-to-all-start.3
  124.3 0.6 divide_multiply_fusion.4
  125.7 10.7 %all-to-all-done.3 = bf16[16,3,16,256]{3,2,1,0:T(8,128)(2,1)S(1)} async-done(((bf16[16,3,16,256]{3,2,1,0:T(8,128)(2,1)}), bf16[16,3,16,256]{3,2,1,0:T(8,128)(2,1)S(1)}, u32[]{:S(2)}, u32[]{:S(2)}) %all-to-all-start.3) | async-done | bytes 393248 | tf_op jit(solution)/shard_map/all_to_all | solution.py:78
  137.0 3.7 %fusion.68 = f32[48,16,256]{2,1,0:T(8,128)S(1)} fusion(bf16[48,256,256]{2,1,0:T(8,128)(2,1)} %param.29, bf16[48,16,256]{2,1,0:T(8,128)(2,1)S(1)} %gather_fusion.4, pred[48]{0:T(512)(128)(4,1)S(1)} %get-tuple-element.10), kind=kOutput, calls=%fused_computation.92 | convolution fusion | flops 100859904 | bytes 7471152 | tf_op jit(solution)/shard_map/ltp,lpq->ltq/dot_general | solution.py:92
  140.7 1.0 convert_reduce_fusion.3
  142.4 0.6 gather_fusion.6
  143.0 31.4 %psum.44 = f32[8,16]{1,0:T(8,128)S(1)} all-reduce(f32[8,16]{1,0:T(8,128)S(1)} %broadcast_select_fusion.9), channel_id=1, replica_groups=mesh['runs'=2,'area'=16] {'area'}, use_global_device_ids=true, to_apply=%region_14.18 | all-reduce | flops 128 | bytes 1024 | tf_op jit(solution)/shard_map/psum | solution.py:85
  174.6 0.9 broadcast_select_fusion.3
  175.4 3.6 all-to-all-start.4
  179.0 0.6 divide_multiply_fusion.3
  180.4 10.7 %all-to-all-done.4 = bf16[16,3,16,256]{3,2,1,0:T(8,128)(2,1)S(1)} async-done(((bf16[16,3,16,256]{3,2,1,0:T(8,128)(2,1)}), bf16[16,3,16,256]{3,2,1,0:T(8,128)(2,1)S(1)}, u32[]{:S(2)}, u32[]{:S(2)}) %all-to-all-start.4) | async-done | bytes 393248 | tf_op jit(solution)/shard_map/all_to_all | solution.py:78
  191.7 3.7 %fusion.66 = f32[48,16,256]{2,1,0:T(8,128)S(1)} fusion(bf16[48,256,256]{2,1,0:T(8,128)(2,1)} %param.29, bf16[48,16,256]{2,1,0:T(8,128)(2,1)S(1)} %gather_fusion.7, pred[48]{0:T(512)(128)(4,1)S(1)} %get-tuple-element.10), kind=kOutput, calls=%fused_computation.90 | convolution fusion | flops 100859904 | bytes 7471152 | tf_op jit(solution)/shard_map/ltp,lpq->ltq/dot_general | solution.py:92
  195.5 1.0 convert_reduce_fusion.2
  197.1 0.6 gather_fusion.9
  197.8 31.4 %psum.45 = f32[8,16]{1,0:T(8,128)S(1)} all-reduce(f32[8,16]{1,0:T(8,128)S(1)} %broadcast_select_fusion.8), channel_id=1, replica_groups=mesh['runs'=2,'area'=16] {'area'}, use_global_device_ids=true, to_apply=%region_17.21 | all-reduce | flops 128 | bytes 1024 | tf_op jit(solution)/shard_map/psum | solution.py:85
  229.3 0.9 broadcast_select_fusion.2
  230.2 3.7 %all-to-all-start.5 = ((bf16[16,3,16,256]{3,2,1,0:T(8,128)(2,1)}), bf16[16,3,16,256]{3,2,1,0:T(8,128)(2,1)S(1)}, u32[]{:S(2)}, u32[]{:S(2)}) async-start(bf16[16,3,16,256]{3,2,1,0:T(8,128)(2,1)} %bitcast.18), calls=%async_computation.5 | async-start | bytes 786432 | tf_op jit(solution)/shard_map/all_to_all | solution.py:78
  233.9 0.6 divide_multiply_fusion.2
  235.3 10.5 %all-to-all-done.5 = bf16[16,3,16,256]{3,2,1,0:T(8,128)(2,1)S(1)} async-done(((bf16[16,3,16,256]{3,2,1,0:T(8,128)(2,1)}), bf16[16,3,16,256]{3,2,1,0:T(8,128)(2,1)S(1)}, u32[]{:S(2)}, u32[]{:S(2)}) %all-to-all-start.5) | async-done | bytes 393248 | tf_op jit(solution)/shard_map/all_to_all | solution.py:78
  246.5 3.7 %fusion.64 = f32[48,16,256]{2,1,0:T(8,128)S(1)} fusion(bf16[48,256,256]{2,1,0:T(8,128)(2,1)} %param.29, bf16[48,16,256]{2,1,0:T(8,128)(2,1)S(1)} %gather_fusion.10, pred[48]{0:T(512)(128)(4,1)S(1)} %get-tuple-element.10), kind=kOutput, calls=%fused_computation.88 | convolution fusion | flops 100859904 | bytes 7471152 | tf_op jit(solution)/shard_map/ltp,lpq->ltq/dot_general | solution.py:92
  250.2 1.0 convert_reduce_fusion.1
  252.5 31.4 %psum.46 = f32[8,16]{1,0:T(8,128)S(1)} all-reduce(f32[8,16]{1,0:T(8,128)S(1)} %broadcast_select_fusion.7), channel_id=1, replica_groups=mesh['runs'=2,'area'=16] {'area'}, use_global_device_ids=true, to_apply=%region_20.24 | all-reduce | flops 128 | bytes 1024 | tf_op jit(solution)/shard_map/psum | solution.py:85
  284.0 0.9 broadcast_select_fusion.1
  284.9 3.6 all-to-all-start.6
  288.5 0.6 divide_multiply_fusion.1
  289.9 10.7 %all-to-all-done.6 = bf16[16,3,16,256]{3,2,1,0:T(8,128)(2,1)S(1)} async-done(((bf16[16,3,16,256]{3,2,1,0:T(8,128)(2,1)}), bf16[16,3,16,256]{3,2,1,0:T(8,128)(2,1)S(1)}, u32[]{:S(2)}, u32[]{:S(2)}) %all-to-all-start.6) | async-done | bytes 393248 | tf_op jit(solution)/shard_map/all_to_all | solution.py:78
  301.2 3.7 %fusion.62 = f32[48,16,256]{2,1,0:T(8,128)S(1)} fusion(bf16[48,256,256]{2,1,0:T(8,128)(2,1)} %param.29, bf16[48,16,256]{2,1,0:T(8,128)(2,1)S(1)} %gather_fusion.13, pred[48]{0:T(512)(128)(4,1)S(1)} %get-tuple-element.10), kind=kOutput, calls=%fused_computation.86 | convolution fusion | flops 100859904 | bytes 7471152 | tf_op jit(solution)/shard_map/ltp,lpq->ltq/dot_general | solution.py:92
  305.0 1.0 convert_reduce_fusion
  307.2 31.4 %psum.47 = f32[8,16]{1,0:T(8,128)S(1)} all-reduce(f32[8,16]{1,0:T(8,128)S(1)} %broadcast_select_fusion.6), channel_id=1, replica_groups=mesh['runs'=2,'area'=16] {'area'}, use_global_device_ids=true, to_apply=%region_23.27 | all-reduce | flops 128 | bytes 1024 | tf_op jit(solution)/shard_map/psum | solution.py:85
  338.8 0.9 broadcast_select_fusion
  339.6 3.6 all-to-all-start.7
  343.2 0.6 divide_multiply_fusion
  344.6 10.7 %all-to-all-done.7 = bf16[16,3,16,256]{3,2,1,0:T(8,128)(2,1)S(1)} async-done(((bf16[16,3,16,256]{3,2,1,0:T(8,128)(2,1)}), bf16[16,3,16,256]{3,2,1,0:T(8,128)(2,1)S(1)}, u32[]{:S(2)}, u32[]{:S(2)}) %all-to-all-start.7) | async-done | bytes 393248 | tf_op jit(solution)/shard_map/all_to_all | solution.py:78
  355.9 3.7 %fusion.60 = f32[48,16,256]{2,1,0:T(8,128)S(1)} fusion(bf16[48,256,256]{2,1,0:T(8,128)(2,1)} %param.29, bf16[48,16,256]{2,1,0:T(8,128)(2,1)S(1)} %gather_fusion.16, pred[48]{0:T(512)(128)(4,1)S(1)} %get-tuple-element.10), kind=kOutput, calls=%fused_computation.84 | convolution fusion | flops 100859904 | bytes 7471152 | tf_op jit(solution)/shard_map/ltp,lpq->ltq/dot_general | solution.py:92
  359.7 0.8 fusion.48
  360.5 0.6 copy.66
  (75 shorter events, 14.6 us)
Async XLA Ops:
  0.0 70.1 %copy-start = (bf16[16,256,256]{2,1,0:T(8,128)(2,1)S(1)}, bf16[16,256,256]{2,1,0:T(8,128)(2,1)}, u32[]{:S(2)}) copy-start(bf16[16,256,256]{2,1,0:T(8,128)(2,1)} %param.33) | copy-start | bytes 6291460
  3.1 51.3 %all-to-all-start.1 = ((s32[16,1,3]{2,1,0:T(1,128)}), s32[16,1,3]{2,1,0:T(1,128)S(1)}, u32[]{:S(2)}, u32[]{:S(2)}) async-start(s32[16,1,3]{2,1,0:T(1,128)} %bitcast.6), calls=%async_computation.1 | async-start | bytes 16384 | tf_op jit(solution)/shard_map/all_to_all | solution.py:50
  54.4 9.9 %all-to-all-start = ((s32[16,1,3]{2,1,0:T(1,128)}), s32[16,1,3]{2,1,0:T(1,128)S(1)}, u32[]{:S(2)}, u32[]{:S(2)}) async-start(s32[16,1,3]{2,1,0:T(1,128)} %bitcast.5), calls=%async_computation | async-start | bytes 16384 | tf_op jit(solution)/shard_map/all_to_all | solution.py:53
  65.1 20.9 %copy-start.2 = (s32[48]{0:T(128)S(1)}, s32[48]{0:T(128)}, u32[]{:S(2)}) copy-start(s32[48]{0:T(128)} %param.27) | copy-start | bytes 580
  65.9 15.7 %all-to-all-start.2 = ((bf16[16,3,16,256]{3,2,1,0:T(8,128)(2,1)}), bf16[16,3,16,256]{3,2,1,0:T(8,128)(2,1)S(1)}, u32[]{:S(2)}, u32[]{:S(2)}) async-start(bf16[16,3,16,256]{3,2,1,0:T(8,128)(2,1)} %bitcast.8), calls=%async_computation.2 | async-start | bytes 786432 | tf_op jit(solution)/shard_map/all_to_all | solution.py:78
  82.2 43.1 %copy-start.1 = (s32[16]{0:T(128)S(1)}, s32[16]{0:T(128)}, u32[]{:S(2)}) copy-start(s32[16]{0:T(128)} %param.31) | copy-start | bytes 196
  120.7 15.7 %all-to-all-start.3 = ((bf16[16,3,16,256]{3,2,1,0:T(8,128)(2,1)}), bf16[16,3,16,256]{3,2,1,0:T(8,128)(2,1)S(1)}, u32[]{:S(2)}, u32[]{:S(2)}) async-start(bf16[16,3,16,256]{3,2,1,0:T(8,128)(2,1)} %bitcast.14), calls=%async_computation.3 | async-start | bytes 786432 | tf_op jit(solution)/shard_map/all_to_all | solution.py:78
  175.4 15.7 %all-to-all-start.4 = ((bf16[16,3,16,256]{3,2,1,0:T(8,128)(2,1)}), bf16[16,3,16,256]{3,2,1,0:T(8,128)(2,1)S(1)}, u32[]{:S(2)}, u32[]{:S(2)}) async-start(bf16[16,3,16,256]{3,2,1,0:T(8,128)(2,1)} %bitcast.16), calls=%async_computation.4 | async-start | bytes 786432 | tf_op jit(solution)/shard_map/all_to_all | solution.py:78
  230.2 15.7 %all-to-all-start.5 = ((bf16[16,3,16,256]{3,2,1,0:T(8,128)(2,1)}), bf16[16,3,16,256]{3,2,1,0:T(8,128)(2,1)S(1)}, u32[]{:S(2)}, u32[]{:S(2)}) async-start(bf16[16,3,16,256]{3,2,1,0:T(8,128)(2,1)} %bitcast.18), calls=%async_computation.5 | async-start | bytes 786432 | tf_op jit(solution)/shard_map/all_to_all | solution.py:78
  284.9 15.7 %all-to-all-start.6 = ((bf16[16,3,16,256]{3,2,1,0:T(8,128)(2,1)}), bf16[16,3,16,256]{3,2,1,0:T(8,128)(2,1)S(1)}, u32[]{:S(2)}, u32[]{:S(2)}) async-start(bf16[16,3,16,256]{3,2,1,0:T(8,128)(2,1)} %bitcast.20), calls=%async_computation.6 | async-start | bytes 786432 | tf_op jit(solution)/shard_map/all_to_all | solution.py:78
  339.6 15.7 %all-to-all-start.7 = ((bf16[16,3,16,256]{3,2,1,0:T(8,128)(2,1)}), bf16[16,3,16,256]{3,2,1,0:T(8,128)(2,1)S(1)}, u32[]{:S(2)}, u32[]{:S(2)}) async-start(bf16[16,3,16,256]{3,2,1,0:T(8,128)(2,1)} %bitcast.22), calls=%async_computation.7 | async-start | bytes 786432 | tf_op jit(solution)/shard_map/all_to_all | solution.py:78
where the time goes:
time: 363 us; the launch traced here: 361 us
  blocking collectives  191 us (53%)
  waiting for transfers between devices  67.9 us (19%)
  matrix products  33.8 us (9%)
  starting transfers between devices  32.4 us (9%)
  other arithmetic  18.7 us (5%)
  local copies, waits for them, and re-layouts  16.2 us (4%)
    psum x6, blocking collectives, local(): summed = lax.psum(area_table, 'area')  191 us
    all_to_all x6, waiting for transfers between devices, local(): lax.all_to_all(outgoing, 'area', split_axis=0, concat_axis=0, tiled=True)  63.5 us
    dot_general x6, matrix products, local(): jnp.einsum('ltp,lpq->ltq', remote_in, remote_weight, preferred_element_ty...  22.5 us
    all_to_all x6, starting transfers between devices, local(): lax.all_to_all(outgoing, 'area', split_axis=0, concat_axis=0, tiled=True)  21.5 us
    all_to_all x1, starting transfers between devices, local(): lax.all_to_all(want_block.reshape(devices, capacity), 'area', split_axis=...  7.39 us
  transfers between devices with their start and end apart: 8, of which 7 were waited for; matrix products, arithmetic and copies ran while one was open for 6% of the time, Pallas kernels for 0%

commit v1 on v0

--- a/solution.py
+++ b/solution.py
@@ -82,7 +82,9 @@
         previous = state_rows[:blocks].astype(jnp.float32)
         own_sum = jnp.sum(previous, axis=(0, 2))
         area_table = jnp.where(area_mask[:, None], own_sum[None, :], 0.0)
-        summed = lax.psum(area_table, "area")
+        summed = area_table
+        for hop in (1, 2, 4, 8):
+            summed = summed + lax.ppermute(summed, "area", [(dev, dev ^ hop) for dev in range(16)])
         total_mine = jnp.sum(jnp.where(area_mask[:, None], summed, 0.0), axis=0)
         mean_now = total_mine / area_count
         local_in = jnp.take(state_rows, local_index, axis=0)

time: 363 us -> 198 us (0.55)
  blocking collectives: 191 us -> 0 us
  starting transfers between devices: 32.4 us -> 84.4 us
  waiting for transfers between devices: 67.9 us -> 43.6 us
    psum x6 -> x0, blocking collectives: 191 us -> none  [local(): summed = lax.psum(area_table, 'area')]
    all_to_all x6, waiting for transfers between devices: 63.5 us -> 0.02 us  [local(): lax.all_to_all(outgoing, 'area', split_axis=0, concat_axis=0, tiled=True)]
    ppermute x0 -> x24, starting transfers between devices: none -> 46.5 us  [local(): lax.ppermute(summed, 'area', [(dev, dev ^ hop) for dev in range(16)])]
    ppermute x0 -> x24, waiting for transfers between devices: none -> 39.1 us  [local(): lax.ppermute(summed, 'area', [(dev, dev ^ hop) for dev in range(16)])]
  transfers between devices with their start and end apart: 8 -> 32, of which waited for: 7 -> 13; matrix products, arithmetic and copies ran while one was open for 6% -> 16% of each run, Pallas kernels for 0% -> 0%
where the time goes in v1:
time: 198 us; the launch traced here: 197 us
  starting transfers between devices  84.4 us (43%)
  waiting for transfers between devices  43.6 us (22%)
  matrix products  33.7 us (17%)
  other arithmetic  18.8 us (9%)
  local copies, waits for them, and re-layouts  15.4 us (8%)
    ppermute x24, starting transfers between devices, local(): lax.ppermute(summed, 'area', [(dev, dev ^ hop) for dev in range(16)])  46.5 us
    ppermute x24, waiting for transfers between devices, local(): lax.ppermute(summed, 'area', [(dev, dev ^ hop) for dev in range(16)])  39.1 us
    all_to_all x6, starting transfers between devices, local(): lax.all_to_all(outgoing, 'area', split_axis=0, concat_axis=0, tiled=True)  24.7 us
    dot_general x6, matrix products, local(): jnp.einsum('ltp,lpq->ltq', remote_in, remote_weight, preferred_element_ty...  22.5 us
    all_to_all x1, starting transfers between devices, local(): lax.all_to_all(want_block.reshape(devices, capacity), 'area', split_axis=...  7.39 us
    dot_general x6, matrix products, local(): jnp.einsum('bl,ltq->btq', target_onehot, remote_terms, precision=lax.Prec...  5.92 us
    all_to_all x1, starting transfers between devices, local(): lax.all_to_all(want_delay.reshape(devices, capacity), 'area', split_axis=...  5.76 us
    select_n x7, other arithmetic, local(): jnp.take(state_rows, (asked_delay - 1) * blocks + asked_block, axis=0)  5.15 us
  transfers between devices with their start and end apart: 32, of which 13 were waited for; matrix products, arithmetic and copies ran while one was open for 16% of the time, Pallas kernels for 0%

profile of v1, /device:TPU:0, one launch (start us, length us, event | category | flops | bytes accessed | tf_op | source)
XLA Modules:
  0.0 197.2 jit_solution(11606033375594691733)
XLA Ops:
  0.0 1.0 convert_reduce_fusion.5
  1.7 0.8 select_reduce_fusion.1
  2.4 0.7 all_to_all.29
  3.1 7.4 %all-to-all-start.1 = ((s32[16,1,3]{2,1,0:T(1,128)}), s32[16,1,3]{2,1,0:T(1,128)S(1)}, u32[]{:S(2)}, u32[]{:S(2)}) async-start(s32[16,1,3]{2,1,0:T(1,128)} %bitcast.6), calls=%async_computation.1 | async-start | bytes 16384 | tf_op jit(solution)/shard_map/all_to_all | solution.py:50
  10.5 1.3 dynamic_slice.3
  12.4 0.8 fusion.161
  15.4 0.7 broadcast_in_dim_reshape.3
  17.1 1.0 fusion.88
  18.9 5.8 %all-to-all-start = ((s32[16,1,3]{2,1,0:T(1,128)}), s32[16,1,3]{2,1,0:T(1,128)S(1)}, u32[]{:S(2)}, u32[]{:S(2)}) async-start(s32[16,1,3]{2,1,0:T(1,128)} %bitcast.5), calls=%async_computation | async-start | bytes 16384 | tf_op jit(solution)/shard_map/all_to_all | solution.py:53
  24.6 1.9 select_reduce_fusion.8
  26.6 4.5 %all-to-all-done = s32[16,1,3]{2,1,0:T(1,128)S(1)} async-done(((s32[16,1,3]{2,1,0:T(1,128)}), s32[16,1,3]{2,1,0:T(1,128)S(1)}, u32[]{:S(2)}, u32[]{:S(2)}) %all-to-all-start) | async-done | bytes 224 | tf_op jit(solution)/shard_map/all_to_all | solution.py:53
  32.4 0.9 broadcast_select_fusion.5
  33.3 3.6 %all-to-all-start.2 = ((bf16[16,3,16,256]{3,2,1,0:T(8,128)(2,1)}), bf16[16,3,16,256]{3,2,1,0:T(8,128)(2,1)S(1)}, u32[]{:S(2)}, u32[]{:S(2)}) async-start(bf16[16,3,16,256]{3,2,1,0:T(8,128)(2,1)} %bitcast.8), calls=%async_computation.2 | async-start | bytes 786432 | tf_op jit(solution)/shard_map/all_to_all | solution.py:78
  36.9 1.8 collective-permute-start.2
  38.7 5.5 %collective-permute-done.2 = f32[8,16]{1,0:T(8,128)S(1)} collective-permute-done((f32[8,16]{1,0:T(8,128)S(1)}, f32[8,16]{1,0:T(8,128)S(1)}, u32[]{:S(2)}, u32[]{:S(2)}) %collective-permute-start.2) | collective-permute-done | bytes 544 | tf_op jit(solution)/shard_map/ppermute | solution.py:87
  44.2 4.5 %collective-permute-start.3 = (f32[8,16]{1,0:T(8,128)S(1)}, f32[8,16]{1,0:T(8,128)S(1)}, u32[]{:S(2)}, u32[]{:S(2)}) collective-permute-start(f32[8,16]{1,0:T(8,128)S(1)} %add.195), channel_id=1, source_target_pairs={{0,8},{1,9},{2,10},{3,11},{4,12},{5,13},{6,14},{7,15},{8,0},{9,1},... | collective-permute-start | bytes 1544 | tf_op jit(solution)/shard_map/ppermute | solution.py:87
  48.7 1.2 fusion.135
  52.0 3.8 %fusion.70 = f32[48,16,256]{2,1,0:T(8,128)S(1)} fusion(bf16[48,256,256]{2,1,0:T(8,128)(2,1)} %param.29, bf16[48,16,256]{2,1,0:T(8,128)(2,1)S(1)} %gather_fusion.1, pred[48]{0:T(512)(128)(4,1)S(1)} %get-tuple-element.10), kind=kOutput, calls=%fused_computation.94 | convolution fusion | flops 100859904 | bytes 7471152 | tf_op jit(solution)/shard_map/ltp,lpq->ltq/dot_general | solution.py:94
  55.7 1.0 convert_reduce_fusion.4
  58.5 1.5 collective-permute-start.5
  60.0 0.9 broadcast_select_fusion.4
  60.9 3.9 %all-to-all-start.3 = ((bf16[16,3,16,256]{3,2,1,0:T(8,128)(2,1)}), bf16[16,3,16,256]{3,2,1,0:T(8,128)(2,1)S(1)}, u32[]{:S(2)}, u32[]{:S(2)}) async-start(bf16[16,3,16,256]{3,2,1,0:T(8,128)(2,1)} %bitcast.14), calls=%async_computation.3 | async-start | bytes 786432 | tf_op jit(solution)/shard_map/all_to_all | solution.py:78
  64.9 1.9 collective-permute-start.6
  67.2 5.1 %collective-permute-done.6 = f32[8,16]{1,0:T(8,128)S(1)} collective-permute-done((f32[8,16]{1,0:T(8,128)S(1)}, f32[8,16]{1,0:T(8,128)S(1)}, u32[]{:S(2)}, u32[]{:S(2)}) %collective-permute-start.6) | collective-permute-done | bytes 544 | tf_op jit(solution)/shard_map/ppermute | solution.py:87
  72.3 4.4 %collective-permute-start.7 = (f32[8,16]{1,0:T(8,128)S(1)}, f32[8,16]{1,0:T(8,128)S(1)}, u32[]{:S(2)}, u32[]{:S(2)}) collective-permute-start(f32[8,16]{1,0:T(8,128)S(1)} %add.203), channel_id=1, source_target_pairs={{0,8},{1,9},{2,10},{3,11},{4,12},{5,13},{6,14},{7,15},{8,0},{9,1},... | collective-permute-start | bytes 1544 | tf_op jit(solution)/shard_map/ppermute | solution.py:87
  76.8 1.6 collective-permute-done.7
  79.7 3.7 %fusion.68 = f32[48,16,256]{2,1,0:T(8,128)S(1)} fusion(bf16[48,256,256]{2,1,0:T(8,128)(2,1)} %param.29, bf16[48,16,256]{2,1,0:T(8,128)(2,1)S(1)} %gather_fusion.4, pred[48]{0:T(512)(128)(4,1)S(1)} %get-tuple-element.10), kind=kOutput, calls=%fused_computation.92 | convolution fusion | flops 100859904 | bytes 7471152 | tf_op jit(solution)/shard_map/ltp,lpq->ltq/dot_general | solution.py:94
  83.4 1.0 convert_reduce_fusion.3
  86.3 1.5 collective-permute-start.9
  87.7 0.9 broadcast_select_fusion.3
  88.6 4.3 %all-to-all-start.4 = ((bf16[16,3,16,256]{3,2,1,0:T(8,128)(2,1)}), bf16[16,3,16,256]{3,2,1,0:T(8,128)(2,1)S(1)}, u32[]{:S(2)}, u32[]{:S(2)}) async-start(bf16[16,3,16,256]{3,2,1,0:T(8,128)(2,1)} %bitcast.16), calls=%async_computation.4 | async-start | bytes 786432 | tf_op jit(solution)/shard_map/all_to_all | solution.py:78
  93.0 1.9 collective-permute-start.10
  95.3 5.1 %collective-permute-done.10 = f32[8,16]{1,0:T(8,128)S(1)} collective-permute-done((f32[8,16]{1,0:T(8,128)S(1)}, f32[8,16]{1,0:T(8,128)S(1)}, u32[]{:S(2)}, u32[]{:S(2)}) %collective-permute-start.10) | collective-permute-done | bytes 544 | tf_op jit(solution)/shard_map/ppermute | solution.py:87
  100.4 4.4 %collective-permute-start.11 = (f32[8,16]{1,0:T(8,128)S(1)}, f32[8,16]{1,0:T(8,128)S(1)}, u32[]{:S(2)}, u32[]{:S(2)}) collective-permute-start(f32[8,16]{1,0:T(8,128)S(1)} %add.211), channel_id=1, source_target_pairs={{0,8},{1,9},{2,10},{3,11},{4,12},{5,13},{6,14},{7,15},{8,0},{9,1},... | collective-permute-start | bytes 1544 | tf_op jit(solution)/shard_map/ppermute | solution.py:87
  104.9 1.6 collective-permute-done.11
  107.7 3.7 %fusion.66 = f32[48,16,256]{2,1,0:T(8,128)S(1)} fusion(bf16[48,256,256]{2,1,0:T(8,128)(2,1)} %param.29, bf16[48,16,256]{2,1,0:T(8,128)(2,1)S(1)} %gather_fusion.7, pred[48]{0:T(512)(128)(4,1)S(1)} %get-tuple-element.10), kind=kOutput, calls=%fused_computation.90 | convolution fusion | flops 100859904 | bytes 7471152 | tf_op jit(solution)/shard_map/ltp,lpq->ltq/dot_general | solution.py:94
  111.5 1.0 convert_reduce_fusion.2
  114.3 1.5 collective-permute-start.13
  115.8 0.9 broadcast_select_fusion.2
  116.6 4.3 %all-to-all-start.5 = ((bf16[16,3,16,256]{3,2,1,0:T(8,128)(2,1)}), bf16[16,3,16,256]{3,2,1,0:T(8,128)(2,1)S(1)}, u32[]{:S(2)}, u32[]{:S(2)}) async-start(bf16[16,3,16,256]{3,2,1,0:T(8,128)(2,1)} %bitcast.18), calls=%async_computation.5 | async-start | bytes 786432 | tf_op jit(solution)/shard_map/all_to_all | solution.py:78
  121.0 1.9 collective-permute-start.14
  123.3 5.1 %collective-permute-done.14 = f32[8,16]{1,0:T(8,128)S(1)} collective-permute-done((f32[8,16]{1,0:T(8,128)S(1)}, f32[8,16]{1,0:T(8,128)S(1)}, u32[]{:S(2)}, u32[]{:S(2)}) %collective-permute-start.14) | collective-permute-done | bytes 544 | tf_op jit(solution)/shard_map/ppermute | solution.py:87
  128.4 4.4 %collective-permute-start.15 = (f32[8,16]{1,0:T(8,128)S(1)}, f32[8,16]{1,0:T(8,128)S(1)}, u32[]{:S(2)}, u32[]{:S(2)}) collective-permute-start(f32[8,16]{1,0:T(8,128)S(1)} %add.219), channel_id=1, source_target_pairs={{0,8},{1,9},{2,10},{3,11},{4,12},{5,13},{6,14},{7,15},{8,0},{9,1},... | collective-permute-start | bytes 1544 | tf_op jit(solution)/shard_map/ppermute | solution.py:87
  132.9 1.6 collective-permute-done.15
  135.8 3.7 %fusion.64 = f32[48,16,256]{2,1,0:T(8,128)S(1)} fusion(bf16[48,256,256]{2,1,0:T(8,128)(2,1)} %param.29, bf16[48,16,256]{2,1,0:T(8,128)(2,1)S(1)} %gather_fusion.10, pred[48]{0:T(512)(128)(4,1)S(1)} %get-tuple-element.10), kind=kOutput, calls=%fused_computation.88 | convolution fusion | flops 100859904 | bytes 7471152 | tf_op jit(solution)/shard_map/ltp,lpq->ltq/dot_general | solution.py:94
  139.5 1.0 convert_reduce_fusion.1
  142.3 1.5 collective-permute-start.17
  143.8 0.9 broadcast_select_fusion.1
  144.7 4.3 %all-to-all-start.6 = ((bf16[16,3,16,256]{3,2,1,0:T(8,128)(2,1)}), bf16[16,3,16,256]{3,2,1,0:T(8,128)(2,1)S(1)}, u32[]{:S(2)}, u32[]{:S(2)}) async-start(bf16[16,3,16,256]{3,2,1,0:T(8,128)(2,1)} %bitcast.20), calls=%async_computation.6 | async-start | bytes 786432 | tf_op jit(solution)/shard_map/all_to_all | solution.py:78
  149.1 1.9 collective-permute-start.18
  151.4 5.1 %collective-permute-done.18 = f32[8,16]{1,0:T(8,128)S(1)} collective-permute-done((f32[8,16]{1,0:T(8,128)S(1)}, f32[8,16]{1,0:T(8,128)S(1)}, u32[]{:S(2)}, u32[]{:S(2)}) %collective-permute-start.18) | collective-permute-done | bytes 544 | tf_op jit(solution)/shard_map/ppermute | solution.py:87
  156.5 4.4 %collective-permute-start.19 = (f32[8,16]{1,0:T(8,128)S(1)}, f32[8,16]{1,0:T(8,128)S(1)}, u32[]{:S(2)}, u32[]{:S(2)}) collective-permute-start(f32[8,16]{1,0:T(8,128)S(1)} %add.227), channel_id=1, source_target_pairs={{0,8},{1,9},{2,10},{3,11},{4,12},{5,13},{6,14},{7,15},{8,0},{9,1},... | collective-permute-start | bytes 1544 | tf_op jit(solution)/shard_map/ppermute | solution.py:87
  160.9 1.6 collective-permute-done.19
  163.8 3.7 %fusion.62 = f32[48,16,256]{2,1,0:T(8,128)S(1)} fusion(bf16[48,256,256]{2,1,0:T(8,128)(2,1)} %param.29, bf16[48,16,256]{2,1,0:T(8,128)(2,1)S(1)} %gather_fusion.13, pred[48]{0:T(512)(128)(4,1)S(1)} %get-tuple-element.10), kind=kOutput, calls=%fused_computation.86 | convolution fusion | flops 100859904 | bytes 7471152 | tf_op jit(solution)/shard_map/ltp,lpq->ltq/dot_general | solution.py:94
  167.6 1.0 convert_reduce_fusion
  169.9 1.5 collective-permute-start.21
  171.4 0.9 broadcast_select_fusion
  172.8 4.3 %all-to-all-start.7 = ((bf16[16,3,16,256]{3,2,1,0:T(8,128)(2,1)}), bf16[16,3,16,256]{3,2,1,0:T(8,128)(2,1)S(1)}, u32[]{:S(2)}, u32[]{:S(2)}) async-start(bf16[16,3,16,256]{3,2,1,0:T(8,128)(2,1)} %bitcast.22), calls=%async_computation.7 | async-start | bytes 786432 | tf_op jit(solution)/shard_map/all_to_all | solution.py:78
  177.2 1.9 collective-permute-start.22
  179.6 5.1 %collective-permute-done.22 = f32[8,16]{1,0:T(8,128)S(1)} collective-permute-done((f32[8,16]{1,0:T(8,128)S(1)}, f32[8,16]{1,0:T(8,128)S(1)}, u32[]{:S(2)}, u32[]{:S(2)}) %collective-permute-start.22) | collective-permute-done | bytes 544 | tf_op jit(solution)/shard_map/ppermute | solution.py:87
  184.6 4.4 %collective-permute-start.23 = (f32[8,16]{1,0:T(8,128)S(1)}, f32[8,16]{1,0:T(8,128)S(1)}, u32[]{:S(2)}, u32[]{:S(2)}) collective-permute-start(f32[8,16]{1,0:T(8,128)S(1)} %add.235), channel_id=1, source_target_pairs={{0,8},{1,9},{2,10},{3,11},{4,12},{5,13},{6,14},{7,15},{8,0},{9,1},... | collective-permute-start | bytes 1544 | tf_op jit(solution)/shard_map/ppermute | solution.py:87
  189.4 1.2 collective-permute-done.23
  192.0 3.7 %fusion.60 = f32[48,16,256]{2,1,0:T(8,128)S(1)} fusion(bf16[48,256,256]{2,1,0:T(8,128)(2,1)} %param.29, bf16[48,16,256]{2,1,0:T(8,128)(2,1)S(1)} %gather_fusion.16, pred[48]{0:T(512)(128)(4,1)S(1)} %get-tuple-element.10), kind=kOutput, calls=%fused_computation.84 | convolution fusion | flops 100859904 | bytes 7471152 | tf_op jit(solution)/shard_map/ltp,lpq->ltq/dot_general | solution.py:94
  195.7 0.8 fusion.48
  (139 shorter events, 26.5 us)
Async XLA Ops:
  0.0 16.7 %copy-start = (bf16[16,256,256]{2,1,0:T(8,128)(2,1)S(1)}, bf16[16,256,256]{2,1,0:T(8,128)(2,1)}, u32[]{:S(2)}) copy-start(bf16[16,256,256]{2,1,0:T(8,128)(2,1)} %param.33) | copy-start | bytes 6291460
  0.0 48.7 %copy-start.4 = (s32[16]{0:T(128)S(1)}, s32[16]{0:T(128)}, u32[]{:S(2)}) copy-start(s32[16]{0:T(128)} %param.24) | copy-start | bytes 196
  0.0 49.9 %copy-start.1 = (bf16[16,1024]{1,0:T(8,128)(2,1)S(1)}, bf16[16,1024]{1,0:T(8,128)(2,1)}, u32[]{:S(2)}) copy-start(bf16[16,1024]{1,0:T(8,128)(2,1)} %param.21) | copy-start | bytes 98308
  3.1 15.7 %all-to-all-start.1 = ((s32[16,1,3]{2,1,0:T(1,128)}), s32[16,1,3]{2,1,0:T(1,128)S(1)}, u32[]{:S(2)}, u32[]{:S(2)}) async-start(s32[16,1,3]{2,1,0:T(1,128)} %bitcast.6), calls=%async_computation.1 | async-start | bytes 16384 | tf_op jit(solution)/shard_map/all_to_all | solution.py:50
  13.6 18.3 %collective-permute-start = (f32[8,16]{1,0:T(8,128)S(1)}, f32[8,16]{1,0:T(8,128)S(1)}, u32[]{:S(2)}, u32[]{:S(2)}) collective-permute-start(f32[8,16]{1,0:T(8,128)S(1)} %broadcast_select_fusion.11), channel_id=1, source_target_pairs={{0,1},{1,0},{2,3},{3,2},{4,5},{5,4},{6,7},{7,6},{8,9},{9,8},{10,11... | collective-permute-start | bytes 1544 | tf_op jit(solution)/shard_map/ppermute | solution.py:87
  17.1 38.6 %copy-start.3 = (s32[48]{0:T(128)S(1)}, s32[48]{0:T(128)}, u32[]{:S(2)}) copy-start(s32[48]{0:T(128)} %param.27) | copy-start | bytes 580
  18.9 12.2 %all-to-all-start = ((s32[16,1,3]{2,1,0:T(1,128)}), s32[16,1,3]{2,1,0:T(1,128)S(1)}, u32[]{:S(2)}, u32[]{:S(2)}) async-start(s32[16,1,3]{2,1,0:T(1,128)} %bitcast.5), calls=%async_computation | async-start | bytes 16384 | tf_op jit(solution)/shard_map/all_to_all | solution.py:53
  31.9 4.9 %collective-permute-start.1 = (f32[8,16]{1,0:T(8,128)S(1)}, f32[8,16]{1,0:T(8,128)S(1)}, u32[]{:S(2)}, u32[]{:S(2)}) collective-permute-start(f32[8,16]{1,0:T(8,128)S(1)} %fusion.129), channel_id=1, source_target_pairs={{0,2},{1,3},{2,0},{3,1},{4,6},{5,7},{6,4},{7,5},{8,10},{9,11},{10,... | collective-permute-start | bytes 1544 | tf_op jit(solution)/shard_map/ppermute | solution.py:87
  33.3 18.1 %all-to-all-start.2 = ((bf16[16,3,16,256]{3,2,1,0:T(8,128)(2,1)}), bf16[16,3,16,256]{3,2,1,0:T(8,128)(2,1)S(1)}, u32[]{:S(2)}, u32[]{:S(2)}) async-start(bf16[16,3,16,256]{3,2,1,0:T(8,128)(2,1)} %bitcast.8), calls=%async_computation.2 | async-start | bytes 786432 | tf_op jit(solution)/shard_map/all_to_all | solution.py:78
  36.9 7.3 %collective-permute-start.2 = (f32[8,16]{1,0:T(8,128)S(1)}, f32[8,16]{1,0:T(8,128)S(1)}, u32[]{:S(2)}, u32[]{:S(2)}) collective-permute-start(f32[8,16]{1,0:T(8,128)S(1)} %fusion.179), channel_id=1, source_target_pairs={{0,4},{1,5},{2,6},{3,7},{4,0},{5,1},{6,2},{7,3},{8,12},{9,13},{10,... | collective-permute-start | bytes 1544 | tf_op jit(solution)/shard_map/ppermute | solution.py:87
  44.2 6.4 %collective-permute-start.3 = (f32[8,16]{1,0:T(8,128)S(1)}, f32[8,16]{1,0:T(8,128)S(1)}, u32[]{:S(2)}, u32[]{:S(2)}) collective-permute-start(f32[8,16]{1,0:T(8,128)S(1)} %add.195), channel_id=1, source_target_pairs={{0,8},{1,9},{2,10},{3,11},{4,12},{5,13},{6,14},{7,15},{8,0},{9,1},... | collective-permute-start | bytes 1544 | tf_op jit(solution)/shard_map/ppermute | solution.py:87
  52.0 14.9 %copy-start.2 = (s32[16]{0:T(128)S(1)}, s32[16]{0:T(128)}, u32[]{:S(2)}) copy-start(s32[16]{0:T(128)} %param.31) | copy-start | bytes 196
  56.8 1.6 collective-permute-start.4
  58.5 6.3 %collective-permute-start.5 = (f32[8,16]{1,0:T(8,128)S(1)}, f32[8,16]{1,0:T(8,128)S(1)}, u32[]{:S(2)}, u32[]{:S(2)}) collective-permute-start(f32[8,16]{1,0:T(8,128)S(1)} %fusion.130), channel_id=1, source_target_pairs={{0,2},{1,3},{2,0},{3,1},{4,6},{5,7},{6,4},{7,5},{8,10},{9,11},{10,... | collective-permute-start | bytes 1544 | tf_op jit(solution)/shard_map/ppermute | solution.py:87
  60.9 18.2 %all-to-all-start.3 = ((bf16[16,3,16,256]{3,2,1,0:T(8,128)(2,1)}), bf16[16,3,16,256]{3,2,1,0:T(8,128)(2,1)S(1)}, u32[]{:S(2)}, u32[]{:S(2)}) async-start(bf16[16,3,16,256]{3,2,1,0:T(8,128)(2,1)} %bitcast.14), calls=%async_computation.3 | async-start | bytes 786432 | tf_op jit(solution)/shard_map/all_to_all | solution.py:78
  64.9 7.4 %collective-permute-start.6 = (f32[8,16]{1,0:T(8,128)S(1)}, f32[8,16]{1,0:T(8,128)S(1)}, u32[]{:S(2)}, u32[]{:S(2)}) collective-permute-start(f32[8,16]{1,0:T(8,128)S(1)} %fusion.178), channel_id=1, source_target_pairs={{0,4},{1,5},{2,6},{3,7},{4,0},{5,1},{6,2},{7,3},{8,12},{9,13},{10,... | collective-permute-start | bytes 1544 | tf_op jit(solution)/shard_map/ppermute | solution.py:87
  72.3 6.0 %collective-permute-start.7 = (f32[8,16]{1,0:T(8,128)S(1)}, f32[8,16]{1,0:T(8,128)S(1)}, u32[]{:S(2)}, u32[]{:S(2)}) collective-permute-start(f32[8,16]{1,0:T(8,128)S(1)} %add.203), channel_id=1, source_target_pairs={{0,8},{1,9},{2,10},{3,11},{4,12},{5,13},{6,14},{7,15},{8,0},{9,1},... | collective-permute-start | bytes 1544 | tf_op jit(solution)/shard_map/ppermute | solution.py:87
  84.5 1.6 collective-permute-start.8
  86.3 6.6 %collective-permute-start.9 = (f32[8,16]{1,0:T(8,128)S(1)}, f32[8,16]{1,0:T(8,128)S(1)}, u32[]{:S(2)}, u32[]{:S(2)}) collective-permute-start(f32[8,16]{1,0:T(8,128)S(1)} %fusion.131), channel_id=1, source_target_pairs={{0,2},{1,3},{2,0},{3,1},{4,6},{5,7},{6,4},{7,5},{8,10},{9,11},{10,... | collective-permute-start | bytes 1544 | tf_op jit(solution)/shard_map/ppermute | solution.py:87
  88.6 18.6 %all-to-all-start.4 = ((bf16[16,3,16,256]{3,2,1,0:T(8,128)(2,1)}), bf16[16,3,16,256]{3,2,1,0:T(8,128)(2,1)S(1)}, u32[]{:S(2)}, u32[]{:S(2)}) async-start(bf16[16,3,16,256]{3,2,1,0:T(8,128)(2,1)} %bitcast.16), calls=%async_computation.4 | async-start | bytes 786432 | tf_op jit(solution)/shard_map/all_to_all | solution.py:78
  93.0 7.4 %collective-permute-start.10 = (f32[8,16]{1,0:T(8,128)S(1)}, f32[8,16]{1,0:T(8,128)S(1)}, u32[]{:S(2)}, u32[]{:S(2)}) collective-permute-start(f32[8,16]{1,0:T(8,128)S(1)} %fusion.177), channel_id=1, source_target_pairs={{0,4},{1,5},{2,6},{3,7},{4,0},{5,1},{6,2},{7,3},{8,12},{9,13},{10,... | collective-permute-start | bytes 1544 | tf_op jit(solution)/shard_map/ppermute | solution.py:87
  100.4 6.0 %collective-permute-start.11 = (f32[8,16]{1,0:T(8,128)S(1)}, f32[8,16]{1,0:T(8,128)S(1)}, u32[]{:S(2)}, u32[]{:S(2)}) collective-permute-start(f32[8,16]{1,0:T(8,128)S(1)} %add.211), channel_id=1, source_target_pairs={{0,8},{1,9},{2,10},{3,11},{4,12},{5,13},{6,14},{7,15},{8,0},{9,1},... | collective-permute-start | bytes 1544 | tf_op jit(solution)/shard_map/ppermute | solution.py:87
  112.6 1.6 collective-permute-start.12
  114.3 6.6 %collective-permute-start.13 = (f32[8,16]{1,0:T(8,128)S(1)}, f32[8,16]{1,0:T(8,128)S(1)}, u32[]{:S(2)}, u32[]{:S(2)}) collective-permute-start(f32[8,16]{1,0:T(8,128)S(1)} %fusion.132), channel_id=1, source_target_pairs={{0,2},{1,3},{2,0},{3,1},{4,6},{5,7},{6,4},{7,5},{8,10},{9,11},{10,... | collective-permute-start | bytes 1544 | tf_op jit(solution)/shard_map/ppermute | solution.py:87
  116.6 18.6 %all-to-all-start.5 = ((bf16[16,3,16,256]{3,2,1,0:T(8,128)(2,1)}), bf16[16,3,16,256]{3,2,1,0:T(8,128)(2,1)S(1)}, u32[]{:S(2)}, u32[]{:S(2)}) async-start(bf16[16,3,16,256]{3,2,1,0:T(8,128)(2,1)} %bitcast.18), calls=%async_computation.5 | async-start | bytes 786432 | tf_op jit(solution)/shard_map/all_to_all | solution.py:78
  121.0 7.4 %collective-permute-start.14 = (f32[8,16]{1,0:T(8,128)S(1)}, f32[8,16]{1,0:T(8,128)S(1)}, u32[]{:S(2)}, u32[]{:S(2)}) collective-permute-start(f32[8,16]{1,0:T(8,128)S(1)} %fusion.176), channel_id=1, source_target_pairs={{0,4},{1,5},{2,6},{3,7},{4,0},{5,1},{6,2},{7,3},{8,12},{9,13},{10,... | collective-permute-start | bytes 1544 | tf_op jit(solution)/shard_map/ppermute | solution.py:87
  128.4 6.0 %collective-permute-start.15 = (f32[8,16]{1,0:T(8,128)S(1)}, f32[8,16]{1,0:T(8,128)S(1)}, u32[]{:S(2)}, u32[]{:S(2)}) collective-permute-start(f32[8,16]{1,0:T(8,128)S(1)} %add.219), channel_id=1, source_target_pairs={{0,8},{1,9},{2,10},{3,11},{4,12},{5,13},{6,14},{7,15},{8,0},{9,1},... | collective-permute-start | bytes 1544 | tf_op jit(solution)/shard_map/ppermute | solution.py:87
  140.6 1.6 collective-permute-start.16
  142.3 6.6 %collective-permute-start.17 = (f32[8,16]{1,0:T(8,128)S(1)}, f32[8,16]{1,0:T(8,128)S(1)}, u32[]{:S(2)}, u32[]{:S(2)}) collective-permute-start(f32[8,16]{1,0:T(8,128)S(1)} %fusion.133), channel_id=1, source_target_pairs={{0,2},{1,3},{2,0},{3,1},{4,6},{5,7},{6,4},{7,5},{8,10},{9,11},{10,... | collective-permute-start | bytes 1544 | tf_op jit(solution)/shard_map/ppermute | solution.py:87
  144.7 18.6 %all-to-all-start.6 = ((bf16[16,3,16,256]{3,2,1,0:T(8,128)(2,1)}), bf16[16,3,16,256]{3,2,1,0:T(8,128)(2,1)S(1)}, u32[]{:S(2)}, u32[]{:S(2)}) async-start(bf16[16,3,16,256]{3,2,1,0:T(8,128)(2,1)} %bitcast.20), calls=%async_computation.6 | async-start | bytes 786432 | tf_op jit(solution)/shard_map/all_to_all | solution.py:78
  149.1 7.4 %collective-permute-start.18 = (f32[8,16]{1,0:T(8,128)S(1)}, f32[8,16]{1,0:T(8,128)S(1)}, u32[]{:S(2)}, u32[]{:S(2)}) collective-permute-start(f32[8,16]{1,0:T(8,128)S(1)} %fusion.175), channel_id=1, source_target_pairs={{0,4},{1,5},{2,6},{3,7},{4,0},{5,1},{6,2},{7,3},{8,12},{9,13},{10,... | collective-permute-start | bytes 1544 | tf_op jit(solution)/shard_map/ppermute | solution.py:87
  156.5 6.0 %collective-permute-start.19 = (f32[8,16]{1,0:T(8,128)S(1)}, f32[8,16]{1,0:T(8,128)S(1)}, u32[]{:S(2)}, u32[]{:S(2)}) collective-permute-start(f32[8,16]{1,0:T(8,128)S(1)} %add.227), channel_id=1, source_target_pairs={{0,8},{1,9},{2,10},{3,11},{4,12},{5,13},{6,14},{7,15},{8,0},{9,1},... | collective-permute-start | bytes 1544 | tf_op jit(solution)/shard_map/ppermute | solution.py:87
  168.7 1.2 collective-permute-start.20
  169.9 7.2 %collective-permute-start.21 = (f32[8,16]{1,0:T(8,128)S(1)}, f32[8,16]{1,0:T(8,128)S(1)}, u32[]{:S(2)}, u32[]{:S(2)}) collective-permute-start(f32[8,16]{1,0:T(8,128)S(1)} %fusion.134), channel_id=1, source_target_pairs={{0,2},{1,3},{2,0},{3,1},{4,6},{5,7},{6,4},{7,5},{8,10},{9,11},{10,... | collective-permute-start | bytes 1544 | tf_op jit(solution)/shard_map/ppermute | solution.py:87
  172.8 18.6 %all-to-all-start.7 = ((bf16[16,3,16,256]{3,2,1,0:T(8,128)(2,1)}), bf16[16,3,16,256]{3,2,1,0:T(8,128)(2,1)S(1)}, u32[]{:S(2)}, u32[]{:S(2)}) async-start(bf16[16,3,16,256]{3,2,1,0:T(8,128)(2,1)} %bitcast.22), calls=%async_computation.7 | async-start | bytes 786432 | tf_op jit(solution)/shard_map/all_to_all | solution.py:78
  177.2 7.4 %collective-permute-start.22 = (f32[8,16]{1,0:T(8,128)S(1)}, f32[8,16]{1,0:T(8,128)S(1)}, u32[]{:S(2)}, u32[]{:S(2)}) collective-permute-start(f32[8,16]{1,0:T(8,128)S(1)} %fusion.174), channel_id=1, source_target_pairs={{0,4},{1,5},{2,6},{3,7},{4,0},{5,1},{6,2},{7,3},{8,12},{9,13},{10,... | collective-permute-start | bytes 1544 | tf_op jit(solution)/shard_map/ppermute | solution.py:87
  184.6 6.0 %collective-permute-start.23 = (f32[8,16]{1,0:T(8,128)S(1)}, f32[8,16]{1,0:T(8,128)S(1)}, u32[]{:S(2)}, u32[]{:S(2)}) collective-permute-start(f32[8,16]{1,0:T(8,128)S(1)} %add.235), channel_id=1, source_target_pairs={{0,8},{1,9},{2,10},{3,11},{4,12},{5,13},{6,14},{7,15},{8,0},{9,1},... | collective-permute-start | bytes 1544 | tf_op jit(solution)/shard_map/ppermute | solution.py:87
